TPU v7x, 256 devices: a whole 4x4x8 slice. The times are simulated.
256 devices in a mesh: expert: 16 (over x_hi, y, core), blk: 16 (over x_lo, z).
Axes of the slice: x: 4 (x_hi: 2, x_lo: 2; x = x_hi * 2 + x_lo), y: 4, z: 8, core: 2. Of those that a mesh axis runs over, the one named last changes fastest.
Arguments:
- tokens: bfloat16 [2048, 6144], P(('expert', 'blk')), may hold values from -6 to 6
- out_grad: bfloat16 [2048, 6144], P(('expert', 'blk')), may hold values from -6 to 6
- expert_ids: int32 [2048, 4], P(('expert', 'blk')), may hold values from 0 to 15, as said below
- slots: int32 [2048, 4], P(('expert', 'blk')), may hold values from 0 to 2, as said below
- gates: bfloat16 [2048, 4], P(('expert', 'blk')), may hold values from 0.099609375 to 0.59765625
- w_in: bfloat16 [16, 5376, 6144], P('expert', 'blk'), may hold values from -0.078125 to 0.078125
- w_down: bfloat16 [16, 5376, 6144], P('expert', 'blk'), may hold values from -0.078125 to 0.078125
Outputs:
- grad_tokens: bfloat16 [2048, 6144], P(('expert', 'blk'))
- grad_gates: bfloat16 [2048, 4], P(('expert', 'blk'))
Inputs may be any that keep to these rules, and one draw needn't show every extreme that they name: `expert_ids`: within the 8 tokens of one device, a token names 4 different experts, no expert is named more than 3 times, and one expert is named exactly 3 times by every device. Among the entries of one device that name one expert, the slots are 0 to their count minus 1, each once.
All inputs are finite; a program needn't handle non-finite values.
Results may differ from a plain program's by a relative error of at most 0.019.
Values may be sent and summed in bfloat16 or wider, within the bound.
A program may use at most 128 MiB of HBM per device.

v0:
```python
import jax
import jax.numpy as jnp
from jax import lax
from jax.sharding import PartitionSpec as P


def hidden_terms(rows_x, rows_dy, rows_gate, weight_in, weight_down):
    contract = (((1,), (1,)), ((), ()))
    pre = lax.dot_general(rows_x, weight_in, contract, preferred_element_type=jnp.float32)
    back = lax.dot_general(rows_dy, weight_down, contract, preferred_element_type=jnp.float32)
    sigma = jax.nn.sigmoid(pre)
    gate_part = jnp.sum(pre * sigma * back, axis=1)
    slope = rows_gate.astype(jnp.float32)[:, None] * back * sigma * (1.0 + pre * (1.0 - sigma))
    return (slope.astype(jnp.bfloat16), gate_part)


def per_device(tokens, out_grad, expert_ids, slots, gates, w_in, w_down):
    tok_count = tokens.shape[0]
    top_count = expert_ids.shape[1]
    expert_count = lax.axis_size("expert")
    capacity = max(2, (tok_count * top_count + expert_count - 1) // expert_count + 1)
    slot_count = expert_count * capacity
    target = expert_ids * capacity + slots
    matches = (target[None, :, :] == jnp.arange(slot_count, dtype=jnp.int32)[:, None, None]).astype(
        jnp.float32
    )
    placing = jnp.sum(matches, axis=2).astype(jnp.bfloat16)
    send_x = jnp.dot(placing, tokens, preferred_element_type=jnp.float32).astype(jnp.bfloat16)
    send_dy = jnp.dot(placing, out_grad, preferred_element_type=jnp.float32).astype(jnp.bfloat16)
    send_gate = jnp.einsum("stk,tk->s", matches, gates.astype(jnp.float32)).astype(jnp.bfloat16)
    recv_x, recv_dy, recv_gate = (
        lax.all_to_all(send_x, "expert", split_axis=0, concat_axis=0, tiled=True),
        lax.all_to_all(send_dy, "expert", split_axis=0, concat_axis=0, tiled=True),
        lax.all_to_all(send_gate, "expert", split_axis=0, concat_axis=0, tiled=True),
    )
    weight_in = w_in[0]
    weight_down = w_down[0]
    all_x, all_dy, all_gate = (
        lax.all_gather(recv_x, "blk", axis=0, tiled=True),
        lax.all_gather(recv_dy, "blk", axis=0, tiled=True),
        lax.all_gather(recv_gate, "blk", axis=0, tiled=True),
    )
    slope, gate_part = hidden_terms(all_x, all_dy, all_gate, weight_in, weight_down)
    grad_rows = lax.psum_scatter(
        jnp.dot(slope, weight_in, preferred_element_type=jnp.float32).astype(jnp.bfloat16),
        "blk",
        scatter_dimension=0,
        tiled=True,
    )
    gate_rows = lax.psum_scatter(gate_part, "blk", scatter_dimension=0, tiled=True)
    back_rows, back_gate = (
        lax.all_to_all(grad_rows, "expert", split_axis=0, concat_axis=0, tiled=True),
        lax.all_to_all(
            gate_rows.astype(jnp.bfloat16), "expert", split_axis=0, concat_axis=0, tiled=True
        ),
    )
    grad_tokens = lax.dot_general(
        placing, back_rows, (((0,), (0,)), ((), ())), preferred_element_type=jnp.float32
    ).astype(jnp.bfloat16)
    grad_gates = jnp.einsum("stk,s->tk", matches, back_gate.astype(jnp.float32)).astype(
        jnp.bfloat16
    )
    return (grad_tokens, grad_gates)


def solution(mesh):
    return jax.shard_map(
        per_device,
        mesh=mesh,
        in_specs=(
            P(("expert", "blk"), None),
            P(("expert", "blk"), None),
            P(("expert", "blk"), None),
            P(("expert", "blk"), None),
            P(("expert", "blk"), None),
            P("expert", "blk", None),
            P("expert", "blk", None),
        ),
        out_specs=(P(("expert", "blk"), None), P(("expert", "blk"), None)),
        check_vma=False,
    )
```

profile of v0, /device:TPU:1, one launch (start us, length us, event | category | flops | bytes accessed | tf_op | source)
XLA Modules:
  0.0 417.5 jit_solution(10140539445193351380)
XLA Ops:
  7.2 0.0 copy-start
  7.2 0.0 copy-start.2
  7.2 0.0 all-gather.5.cloned.1.call-start
  7.2 0.7 multiply_add_fusion
  8.0 0.1 convert_reduce_fusion
  8.1 0.0 copy-done
  8.1 0.3 convolution_convert_fusion.1
  8.4 0.4 all_to_all.46
  8.8 22.5 %all_to_all.62 = bf16[16,3,6144]{2,1,0:T(4,128)(2,1)S(1)} all-to-all(bf16[16,3,6144]{2,1,0:T(4,128)(2,1)S(1)} %all_to_all.46), channel_id=1, replica_groups=mesh['expert'=16,'blk'=16] {'expert'}, dimensions={0} | all-to-all | bytes 1179648 | tf_op jit(solution)/shard_map/all_to_all | solution.py:32
  31.4 0.0 copy-start.4
  31.4 0.0 copy-start.3
  31.4 1.2 all_to_all.48
  32.6 0.0 all-gather.5.cloned.1.call-update
  32.6 0.0 all-gather.3.cloned.1.call-start
  32.7 0.0 copy-done.2
  32.7 0.3 convolution_convert_fusion.2
  33.0 0.4 all_to_all.43
  33.4 17.8 %all_to_all.63 = bf16[16,3,6144]{2,1,0:T(4,128)(2,1)S(1)} all-to-all(bf16[16,3,6144]{2,1,0:T(4,128)(2,1)S(1)} %all_to_all.43), channel_id=1, replica_groups=mesh['expert'=16,'blk'=16] {'expert'}, dimensions={0} | all-to-all | bytes 1179648 | tf_op jit(solution)/shard_map/all_to_all | solution.py:33
  51.2 1.2 all_to_all.45
  52.4 0.0 all-gather.3.cloned.1.call-update
  52.5 0.0 copy-done.4
  52.5 0.2 fusion.5
  52.7 0.7 all_to_all.55
  53.4 99.0 %all-to-all-start = ((bf16[16,3,1]{1,2,0:T(2,128)(2,1)}), bf16[16,3,1]{1,2,0:T(2,128)(2,1)S(1)}, u32[]{:S(2)}, u32[]{:S(2)}) async-start(bf16[16,3,1]{1,2,0:T(2,128)(2,1)} %all_to_all.55), calls=%async_computation | async-start | bytes 16384 | tf_op jit(solution)/shard_map/all_to_all | solution.py:34
  152.4 0.0 reduce-scatter.2.cloned.1.call-start
  152.5 0.0 copy-done.3
  152.5 0.6 fusion.16
  153.6 5.8 %all-to-all-done = bf16[16,3,1]{1,2,0:T(2,128)(2,1)S(1)} async-done(((bf16[16,3,1]{1,2,0:T(2,128)(2,1)}), bf16[16,3,1]{1,2,0:T(2,128)(2,1)S(1)}, u32[]{:S(2)}, u32[]{:S(2)}) %all-to-all-start) | async-done | bytes 128 | tf_op jit(solution)/shard_map/all_to_all | solution.py:34
  159.4 0.1 reshape.16
  159.6 0.2 dynamic-update-slice
  159.8 32.6 %all-reduce = bf16[768]{0:T(1024)(128)(2,1)S(1)} all-reduce(bf16[768]{0:T(1024)(128)(2,1)S(1)} %dynamic-update-slice), channel_id=1, replica_groups=mesh['expert'=16,'blk'=16] {'blk'}, use_global_device_ids=true, to_apply=%add | all-reduce | flops 768 | bytes 3072
  192.4 0.0 all-gather.5.cloned.1.call-done
  192.4 11.0 %fusion.1 = f32[768,336]{0,1:T(8,128)S(1)} fusion(bf16[768,6144]{1,0:T(8,128)(2,1)} %all-gather.5.cloned.1.call-done, bf16[1,336,6144]{2,1,0:T(8,128)(2,1)} %param.12), kind=kOutput, calls=%fused_computation.5 | convolution fusion | flops 3170893824 | bytes 14598144 | tf_op jit(solution)/shard_map/dot_general | solution.py:9
  203.4 53.5 %all-gather.3.cloned.1.call-done = bf16[768,6144]{1,0:T(8,128)(2,1)} async-done(((bf16[48,6144]{1,0:T(8,128)(2,1)}), bf16[768,6144]{1,0:T(8,128)(2,1)}) %all-gather.3.cloned.1.call-update) | async-done | bytes 9437200 | tf_op jit(solution)/shard_map/all_gather | solution.py:40
  257.0 0.0 copy-start.1
  257.0 11.0 %multiply_reduce_fusion = (f32[768]{0:T(1024)S(1)}, f32[768,336]{0,1:T(8,128)S(1)}) fusion(f32[768,336]{0,1:T(8,128)S(1)} %fusion.1, bf16[768,6144]{1,0:T(8,128)(2,1)} %all-gather.3.cloned.1.call-done, bf16[1,336,6144]{2,1,0:T(8,128)(2,1)} %param.13), kind=kOutput, calls=%fused_computation.11 | convolution fusion | flops 3172441344 | bytes 15633408 | tf_op jit(solution)/shard_map/dot_general | solution.py:10
  268.0 0.0 copy-done.1
  268.0 8.0 %convolution_convert_fusion = bf16[768,6144]{1,0:T(8,128)(2,1)} fusion(bf16[1,336,6144]{2,1,0:T(8,128)(2,1)S(1)} %copy-done.1, f32[768,336]{0,1:T(8,128)S(1)} %fusion.1, f32[768,336]{0,1:T(8,128)S(1)} %get-tuple-element.5, f32[768]{0:T(1024)S(1)} %convert_element_type.38), kind=kOutput, calls=%fused_computation | convolution fusion | flops 3178192896 | bytes 15633408 | tf_op jit(solution)/shard_map/dot_general | solution.py:45
  276.0 0.0 reduce-scatter.2.cloned.1.call-update
  276.7 27.5 %all-reduce.1 = bf16[768]{0:T(1024)(128)(2,1)S(1)} all-reduce(f32[768]{0:T(1024)S(1)} %get-tuple-element.4), channel_id=3, replica_groups=mesh['expert'=16,'blk'=16] {'blk'}, use_global_device_ids=true, to_apply=%region_3.0.clone | all-reduce | flops 768 | bytes 4608
  304.2 0.1 dynamic-slice.4
  304.3 0.7 all_to_all.56
  305.0 12.2 %all-to-all-start.4 = ((bf16[16,3,1]{1,2,0:T(2,128)(2,1)}), bf16[16,3,1]{1,2,0:T(2,128)(2,1)S(1)}, u32[]{:S(2)}, u32[]{:S(2)}) async-start(bf16[16,3,1]{1,2,0:T(2,128)(2,1)} %all_to_all.56), calls=%async_computation.5 | async-start | bytes 16384 | tf_op jit(solution)/shard_map/all_to_all | solution.py:53
  317.2 68.8 %reduce-scatter.2.cloned.1.call-done = bf16[48,6144]{1,0:T(8,128)(2,1)} async-done(((bf16[768,6144]{1,0:T(8,128)(2,1)}), bf16[48,6144]{1,0:T(8,128)(2,1)}) %reduce-scatter.2.cloned.1.call-update) | async-done | bytes 589840 | tf_op jit(solution)/shard_map/reduce_scatter | solution.py:44
  386.0 2.1 all_to_all.49
  388.1 0.0 all-to-all-done.4
  388.1 7.1 %all-to-all-start.3 = ((bf16[16,3,6144]{2,1,0:T(4,128)(2,1)}), bf16[16,3,6144]{2,1,0:T(4,128)(2,1)S(1)}, u32[]{:S(2)}, u32[]{:S(2)}) async-start(bf16[16,3,6144]{2,1,0:T(4,128)(2,1)} %all_to_all.49), calls=%async_computation.4 | async-start | bytes 1572864 | tf_op jit(solution)/shard_map/all_to_all | solution.py:52
  395.2 0.1 reshape.23
  395.3 0.2 fusion.8
  395.5 0.6 convert_element_type.45
  396.1 13.5 %all-to-all-done.3 = bf16[16,3,6144]{2,1,0:T(4,128)(2,1)S(1)} async-done(((bf16[16,3,6144]{2,1,0:T(4,128)(2,1)}), bf16[16,3,6144]{2,1,0:T(4,128)(2,1)S(1)}, u32[]{:S(2)}, u32[]{:S(2)}) %all-to-all-start.3) | async-done | bytes 589856 | tf_op jit(solution)/shard_map/all_to_all | solution.py:52
  409.6 0.5 all_to_all.51
  410.1 0.8 convolution_convert_fusion.3
  (4 shorter events, 0.1 us)
Async XLA Ops:
  7.2 0.9 copy-start
  7.2 25.5 %copy-start.2 = (bf16[8,6144]{1,0:T(8,128)(2,1)S(1)}, bf16[8,6144]{1,0:T(8,128)(2,1)}, u32[]{:S(2)}) copy-start(bf16[8,6144]{1,0:T(8,128)(2,1)} %param.8) | copy-start | bytes 294916
  7.2 185.2 %all-gather.5.cloned.1.call-start = ((), (), s32[]{:S(2)}) async-start(), calls=%async_computation.7 | async-start | bytes 10027008 | tf_op jit(solution)/shard_map/all_gather | solution.py:39
  31.4 21.1 %copy-start.4 = (bf16[8,4]{0,1:T(4,128)(2,1)S(1)}, bf16[8,4]{0,1:T(4,128)(2,1)}, u32[]{:S(2)}) copy-start(bf16[8,4]{0,1:T(4,128)(2,1)} %param.11) | copy-start | bytes 196
  31.4 121.1 %copy-start.3 = (u32[256]{0:T(256)S(1)}, u32[256]{0:T(256)}, u32[]{:S(2)}) copy-start(u32[256]{0:T(256)} %constant.15) | copy-start | bytes 3076
  32.6 224.3 %all-gather.3.cloned.1.call-start = ((), (), s32[]{:S(2)}) async-start(), calls=%async_computation.6 | async-start | bytes 10027008 | tf_op jit(solution)/shard_map/all_gather | solution.py:40
  53.4 106.0 %all-to-all-start = ((bf16[16,3,1]{1,2,0:T(2,128)(2,1)}), bf16[16,3,1]{1,2,0:T(2,128)(2,1)S(1)}, u32[]{:S(2)}, u32[]{:S(2)}) async-start(bf16[16,3,1]{1,2,0:T(2,128)(2,1)} %all_to_all.55), calls=%async_computation | async-start | bytes 16384 | tf_op jit(solution)/shard_map/all_to_all | solution.py:34
  152.4 233.6 %reduce-scatter.2.cloned.1.call-start = ((), (), s32[]{:S(2)}) async-start(), calls=%async_computation.8 | async-start | bytes 10027008 | tf_op jit(solution)/shard_map/reduce_scatter | solution.py:44
  257.0 11.0 %copy-start.1 = (bf16[1,336,6144]{2,1,0:T(8,128)(2,1)S(1)}, bf16[1,336,6144]{2,1,0:T(8,128)(2,1)}, u32[]{:S(2)}) copy-start(bf16[1,336,6144]{2,1,0:T(8,128)(2,1)} %param.12) | copy-start | bytes 12386308
  305.0 83.1 %all-to-all-start.4 = ((bf16[16,3,1]{1,2,0:T(2,128)(2,1)}), bf16[16,3,1]{1,2,0:T(2,128)(2,1)S(1)}, u32[]{:S(2)}, u32[]{:S(2)}) async-start(bf16[16,3,1]{1,2,0:T(2,128)(2,1)} %all_to_all.56), calls=%async_computation.5 | async-start | bytes 16384 | tf_op jit(solution)/shard_map/all_to_all | solution.py:53
  388.1 21.5 %all-to-all-start.3 = ((bf16[16,3,6144]{2,1,0:T(4,128)(2,1)}), bf16[16,3,6144]{2,1,0:T(4,128)(2,1)S(1)}, u32[]{:S(2)}, u32[]{:S(2)}) async-start(bf16[16,3,6144]{2,1,0:T(4,128)(2,1)} %all_to_all.49), calls=%async_computation.4 | async-start | bytes 1572864 | tf_op jit(solution)/shard_map/all_to_all | solution.py:52
Sparse Core Ops, SparseCore 0:
  32.7 110.5 all-gather.4
  145.1 111.8 all-gather.2
  276.2 109.7 reduce-scatter.1
where the time goes:
time: 418 us; the launch traced here: 417 us
  waiting for transfers between devices  142 us (34%)
  starting transfers between devices  118 us (28%)
  blocking collectives  100 us (24%)
  matrix products  32 us (8%)
  between operations  15.1 us (4%)
  local copies, waits for them, and re-layouts  8.4 us (2%)
    all_to_all x1, starting transfers between devices, per_device(): lax.all_to_all(send_gate, 'expert', split_axis=0, concat_axis=0, tiled=True)  99 us
    reduce_scatter x1, waiting for transfers between devices, per_device(): lax.psum_scatter(jnp.dot(slope, weight_in, preferred_element_type=jnp.flo...  68.8 us
    unnamed x2, blocking collectives  60.1 us
    all_gather x1, waiting for transfers between devices, per_device(): lax.all_gather(recv_dy, 'blk', axis=0, tiled=True)  53.5 us
    all_to_all x1, blocking collectives, per_device(): lax.all_to_all(send_x, 'expert', split_axis=0, concat_axis=0, tiled=True)  22.5 us
    all_to_all x1, blocking collectives, per_device(): lax.all_to_all(send_dy, 'expert', split_axis=0, concat_axis=0, tiled=True)  17.8 us
    all_to_all x1, waiting for transfers between devices, per_device(): lax.all_to_all(grad_rows, 'expert', split_axis=0, concat_axis=0, tiled=True)  13.5 us
    all_to_all x1, starting transfers between devices, per_device(): lax.all_to_all(gate_rows.astype(jnp.bfloat16), 'expert', split_axis=0, co...  12.2 us
  transfers between devices with their start and end apart: 6, of which 4 were waited for; matrix products, arithmetic and copies ran while one was open for 3% of the time, Pallas kernels for 0%

commit v1 on v0

--- a/solution.py
+++ b/solution.py
@@ -2,6 +2,14 @@
 import jax.numpy as jnp
 from jax import lax
 from jax.sharding import PartitionSpec as P
+
+
+def _edit_field(field):
+    sheets = []
+    for _ in range(lax.axis_size("blk")):
+        sheets.append(field)
+    long_array = lax.all_to_all(jnp.stack(sheets), split_axis=0, axis_name="blk", concat_axis=0)
+    return jnp.concatenate(long_array, axis=0)
 
 
 def hidden_terms(rows_x, rows_dy, rows_gate, weight_in, weight_down):
@@ -37,7 +45,7 @@
     weight_down = w_down[0]
     all_x, all_dy, all_gate = (
         lax.all_gather(recv_x, "blk", axis=0, tiled=True),
-        lax.all_gather(recv_dy, "blk", axis=0, tiled=True),
+        _edit_field(recv_dy),
         lax.all_gather(recv_gate, "blk", axis=0, tiled=True),
     )
     slope, gate_part = hidden_terms(all_x, all_dy, all_gate, weight_in, weight_down)

time: 418 us -> 583 us (1.39)
  blocking collectives: 100 us -> 282 us
  starting transfers between devices: 118 us -> 39.3 us
  waiting for transfers between devices: 142 us -> 199 us
    unnamed x2, blocking collectives: 60.1 us -> 259 us
    all_to_all x0 -> x2, waiting for transfers between devices: none -> 108 us  [the longest x1 108 us: per_device(): lax.all_to_all(send_dy, 'expert', split_axis=0, concat_axis=0, tiled=True)]
    all_to_all x1, starting transfers between devices: 99 us -> 4.13 us  [per_device(): lax.all_to_all(send_gate, 'expert', split_axis=0, concat_axis=0, tiled=True)]
    all_gather x1 -> x0, waiting for transfers between devices: 53.5 us -> none  [per_device(): lax.all_gather(recv_dy, 'blk', axis=0, tiled=True)]
    all_to_all x1 -> x0, blocking collectives: 17.8 us -> none  [per_device(): lax.all_to_all(send_dy, 'expert', split_axis=0, concat_axis=0, tiled=True)]
    all_to_all x0 -> x2, starting transfers between devices: none -> 11.6 us  [the longest x1 7.17 us: _edit_field(): lax.all_to_all(jnp.stack(sheets), split_axis=0, axis_name='blk', concat_a...]
  transfers between devices with their start and end apart: 6 -> 7, of which waited for: 4 -> 4; matrix products, arithmetic and copies ran while one was open for 3% -> 3% of each run, Pallas kernels for 0% -> 0%
where the time goes in v1:
time: 583 us
  blocking collectives  282 us (48%)
  waiting for transfers between devices  199 us (34%)
  starting transfers between devices  39.3 us (7%)
  matrix products  31.8 us (5%)
  between operations  15.5 us (3%)
  local copies, waits for them, and re-layouts  13.4 us (2%)
    unnamed x2, blocking collectives  259 us
    all_to_all x1, waiting for transfers between devices, per_device(): lax.all_to_all(send_dy, 'expert', split_axis=0, concat_axis=0, tiled=True)  108 us
    reduce_scatter x1, waiting for transfers between devices, per_device(): lax.psum_scatter(jnp.dot(slope, weight_in, preferred_element_type=jnp.flo...  70.9 us
    all_to_all x1, blocking collectives, per_device(): lax.all_to_all(send_x, 'expert', split_axis=0, concat_axis=0, tiled=True)  22.5 us
    all_to_all x1, starting transfers between devices, per_device(): lax.all_to_all(gate_rows.astype(jnp.bfloat16), 'expert', split_axis=0, co...  16.6 us
    all_to_all x1, waiting for transfers between devices, per_device(): lax.all_to_all(grad_rows, 'expert', split_axis=0, concat_axis=0, tiled=True)  13.5 us
  transfers between devices with their start and end apart: 7, of which 4 were waited for; matrix products, arithmetic and copies ran while one was open for 3% of the time, Pallas kernels for 0%

profile of v1, /device:TPU:1, one launch (start us, length us, event | category | flops | bytes accessed | tf_op | source)
XLA Modules:
  0.0 582.6 jit_solution(15878380188504523434)
XLA Ops:
  7.2 0.0 copy-start
  7.2 0.0 copy-start.2
  7.2 0.0 all-gather.2.cloned.1.call-start
  7.2 0.7 multiply_add_fusion
  8.0 0.1 convert_reduce_fusion
  8.0 0.0 copy-done
  8.1 0.3 convolution_convert_fusion.1
  8.4 0.0 copy-start.4
  8.4 0.4 all_to_all.47
  8.8 22.5 %all_to_all.64 = bf16[16,3,6144]{2,1,0:T(4,128)(2,1)S(1)} all-to-all(bf16[16,3,6144]{2,1,0:T(4,128)(2,1)S(1)} %all_to_all.47), channel_id=1, replica_groups=mesh['expert'=16,'blk'=16] {'expert'}, dimensions={0} | all-to-all | bytes 1179648 | tf_op jit(solution)/shard_map/all_to_all | solution.py:40
  31.4 1.2 all_to_all.49
  32.6 0.0 all-gather.2.cloned.1.call-update
  32.6 0.0 copy-done.2
  32.6 0.3 convolution_convert_fusion.2
  33.0 1.1 all_to_all.44
  34.1 4.4 all-to-all-start.1
  38.5 0.0 copy-done.4
  38.5 0.2 fusion.5
  38.7 0.7 all_to_all.56
  39.4 108.4 %all-to-all-done.1 = bf16[16,3,6144]{2,1,0:T(4,128)(2,1)S(1)} async-done(((bf16[16,3,6144]{2,1,0:T(4,128)(2,1)}), bf16[16,3,6144]{2,1,0:T(4,128)(2,1)S(1)}, u32[]{:S(2)}, u32[]{:S(2)}) %all-to-all-start.1) | async-done | bytes 589856 | tf_op jit(solution)/shard_map/all_to_all | solution.py:41
  147.8 4.1 all-to-all-start
  151.9 0.5 stack.4
  152.5 6.5 %all-to-all-done = bf16[16,3,1]{1,2,0:T(2,128)(2,1)S(1)} async-done(((bf16[16,3,1]{1,2,0:T(2,128)(2,1)}), bf16[16,3,1]{1,2,0:T(2,128)(2,1)S(1)}, u32[]{:S(2)}, u32[]{:S(2)}) %all-to-all-start) | async-done | bytes 128 | tf_op jit(solution)/shard_map/all_to_all | solution.py:42
  158.9 4.9 stack.5
  163.8 0.0 copy-start.3
  163.8 7.2 %all-to-all-start.2 = ((bf16[16,48,6144]{2,1,0:T(8,128)(2,1)}), bf16[16,48,6144]{2,1,0:T(8,128)(2,1)}, u32[]{:S(2)}, u32[]{:S(2)}) async-start(bf16[16,48,6144]{2,1,0:T(8,128)(2,1)} %stack.5), calls=%async_computation.2 | async-start | bytes 18874368 | tf_op jit(solution)/shard_map/all_to_all | solution.py:11
  171.0 0.0 reduce-scatter.2.cloned.1.call-start
  171.1 0.0 copy-done.3
  171.1 0.6 fusion.16
  172.3 0.1 reshape.23
  172.5 0.2 dynamic-update-slice
  172.7 234.2 %all-reduce = bf16[768]{0:T(1024)(128)(2,1)S(1)} all-reduce(bf16[768]{0:T(1024)(128)(2,1)S(1)} %dynamic-update-slice), channel_id=1, replica_groups=mesh['expert'=16,'blk'=16] {'blk'}, use_global_device_ids=true, to_apply=%add | all-reduce | flops 768 | bytes 3072
  406.8 0.0 all-gather.2.cloned.1.call-done
  406.9 10.9 %fusion.1 = f32[768,336]{0,1:T(8,128)S(1)} fusion(bf16[768,6144]{1,0:T(8,128)(2,1)} %all-gather.2.cloned.1.call-done, bf16[1,336,6144]{2,1,0:T(8,128)(2,1)} %param.12), kind=kOutput, calls=%fused_computation.5 | convolution fusion | flops 3170893824 | bytes 14598144 | tf_op jit(solution)/shard_map/dot_general | solution.py:17
  417.8 0.0 all-to-all-done.2
  417.8 0.0 copy-start.1
  417.8 11.0 %multiply_reduce_fusion = (f32[768]{0:T(1024)S(1)}, f32[768,336]{0,1:T(8,128)S(1)}) fusion(f32[768,336]{0,1:T(8,128)S(1)} %fusion.1, bf16[768,6144]{1,0:T(8,128)(2,1)} %bitcast.3, bf16[1,336,6144]{2,1,0:T(8,128)(2,1)} %param.13), kind=kOutput, calls=%fused_computation.11 | convolution fusion | flops 3172441344 | bytes 15633408 | tf_op jit(solution)/shard_map/dot_general | solution.py:18
  428.8 0.0 copy-done.1
  428.8 8.0 %convolution_convert_fusion = bf16[768,6144]{1,0:T(8,128)(2,1)} fusion(bf16[1,336,6144]{2,1,0:T(8,128)(2,1)S(1)} %copy-done.1, f32[768,336]{0,1:T(8,128)S(1)} %fusion.1, f32[768,336]{0,1:T(8,128)S(1)} %get-tuple-element.5, f32[768]{0:T(1024)S(1)} %convert_element_type.38), kind=kOutput, calls=%fused_computation | convolution fusion | flops 3178192896 | bytes 15633408 | tf_op jit(solution)/shard_map/dot_general | solution.py:53
  436.8 0.0 reduce-scatter.2.cloned.1.call-update
  437.5 25.1 %all-reduce.1 = bf16[768]{0:T(1024)(128)(2,1)S(1)} all-reduce(f32[768]{0:T(1024)S(1)} %get-tuple-element.4), channel_id=3, replica_groups=mesh['expert'=16,'blk'=16] {'blk'}, use_global_device_ids=true, to_apply=%region_3.0.clone | all-reduce | flops 768 | bytes 4608
  462.6 0.1 dynamic-slice.4
  462.7 0.7 all_to_all.57
  463.4 16.6 %all-to-all-start.5 = ((bf16[16,3,1]{1,2,0:T(2,128)(2,1)}), bf16[16,3,1]{1,2,0:T(2,128)(2,1)S(1)}, u32[]{:S(2)}, u32[]{:S(2)}) async-start(bf16[16,3,1]{1,2,0:T(2,128)(2,1)} %all_to_all.57), calls=%async_computation.6 | async-start | bytes 16384 | tf_op jit(solution)/shard_map/all_to_all | solution.py:61
  480.0 70.9 %reduce-scatter.2.cloned.1.call-done = bf16[48,6144]{1,0:T(8,128)(2,1)} async-done(((bf16[768,6144]{1,0:T(8,128)(2,1)}), bf16[48,6144]{1,0:T(8,128)(2,1)}) %reduce-scatter.2.cloned.1.call-update) | async-done | bytes 589840 | tf_op jit(solution)/shard_map/reduce_scatter | solution.py:52
  551.0 2.1 all_to_all.50
  553.0 0.0 all-to-all-done.5
  553.0 6.9 %all-to-all-start.4 = ((bf16[16,3,6144]{2,1,0:T(4,128)(2,1)}), bf16[16,3,6144]{2,1,0:T(4,128)(2,1)S(1)}, u32[]{:S(2)}, u32[]{:S(2)}) async-start(bf16[16,3,6144]{2,1,0:T(4,128)(2,1)} %all_to_all.50), calls=%async_computation.5 | async-start | bytes 1572864 | tf_op jit(solution)/shard_map/all_to_all | solution.py:60
  560.0 0.1 reshape.30
  560.1 0.2 fusion.8
  560.3 0.6 convert_element_type.45
  560.9 13.5 %all-to-all-done.4 = bf16[16,3,6144]{2,1,0:T(4,128)(2,1)S(1)} async-done(((bf16[16,3,6144]{2,1,0:T(4,128)(2,1)}), bf16[16,3,6144]{2,1,0:T(4,128)(2,1)S(1)}, u32[]{:S(2)}, u32[]{:S(2)}) %all-to-all-start.4) | async-done | bytes 589856 | tf_op jit(solution)/shard_map/all_to_all | solution.py:60
  574.4 0.5 all_to_all.52
  574.9 0.8 convolution_convert_fusion.3
  (4 shorter events, 0.1 us)
Async XLA Ops:
  7.2 0.9 copy-start
  7.2 25.4 %copy-start.2 = (bf16[8,6144]{1,0:T(8,128)(2,1)S(1)}, bf16[8,6144]{1,0:T(8,128)(2,1)}, u32[]{:S(2)}) copy-start(bf16[8,6144]{1,0:T(8,128)(2,1)} %param.8) | copy-start | bytes 294916
  7.2 399.7 %all-gather.2.cloned.1.call-start = ((), (), s32[]{:S(2)}) async-start(), calls=%async_computation.7 | async-start | bytes 10027008 | tf_op jit(solution)/shard_map/all_gather | solution.py:47
  8.4 30.1 %copy-start.4 = (bf16[8,4]{0,1:T(4,128)(2,1)S(1)}, bf16[8,4]{0,1:T(4,128)(2,1)}, u32[]{:S(2)}) copy-start(bf16[8,4]{0,1:T(4,128)(2,1)} %param.11) | copy-start | bytes 196
  34.1 113.7 %all-to-all-start.1 = ((bf16[16,3,6144]{2,1,0:T(4,128)(2,1)}), bf16[16,3,6144]{2,1,0:T(4,128)(2,1)S(1)}, u32[]{:S(2)}, u32[]{:S(2)}) async-start(bf16[16,3,6144]{2,1,0:T(4,128)(2,1)} %all_to_all.44), calls=%async_computation.1 | async-start | bytes 1572864 | tf_op jit(solution)/shard_map/all_to_all | solution.py:41
  147.8 11.1 %all-to-all-start = ((bf16[16,3,1]{1,2,0:T(2,128)(2,1)}), bf16[16,3,1]{1,2,0:T(2,128)(2,1)S(1)}, u32[]{:S(2)}, u32[]{:S(2)}) async-start(bf16[16,3,1]{1,2,0:T(2,128)(2,1)} %all_to_all.56), calls=%async_computation | async-start | bytes 16384 | tf_op jit(solution)/shard_map/all_to_all | solution.py:42
  163.8 7.2 %copy-start.3 = (u32[256]{0:T(256)S(1)}, u32[256]{0:T(256)}, u32[]{:S(2)}) copy-start(u32[256]{0:T(256)} %constant.15) | copy-start | bytes 3076
  163.8 253.9 %all-to-all-start.2 = ((bf16[16,48,6144]{2,1,0:T(8,128)(2,1)}), bf16[16,48,6144]{2,1,0:T(8,128)(2,1)}, u32[]{:S(2)}, u32[]{:S(2)}) async-start(bf16[16,48,6144]{2,1,0:T(8,128)(2,1)} %stack.5), calls=%async_computation.2 | async-start | bytes 18874368 | tf_op jit(solution)/shard_map/all_to_all | solution.py:11
  171.0 380.0 %reduce-scatter.2.cloned.1.call-start = ((), (), s32[]{:S(2)}) async-start(), calls=%async_computation.8 | async-start | bytes 10027008 | tf_op jit(solution)/shard_map/reduce_scatter | solution.py:52
  417.8 11.1 %copy-start.1 = (bf16[1,336,6144]{2,1,0:T(8,128)(2,1)S(1)}, bf16[1,336,6144]{2,1,0:T(8,128)(2,1)}, u32[]{:S(2)}) copy-start(bf16[1,336,6144]{2,1,0:T(8,128)(2,1)} %param.12) | copy-start | bytes 12386308
  463.4 89.6 %all-to-all-start.5 = ((bf16[16,3,1]{1,2,0:T(2,128)(2,1)}), bf16[16,3,1]{1,2,0:T(2,128)(2,1)S(1)}, u32[]{:S(2)}, u32[]{:S(2)}) async-start(bf16[16,3,1]{1,2,0:T(2,128)(2,1)} %all_to_all.57), calls=%async_computation.6 | async-start | bytes 16384 | tf_op jit(solution)/shard_map/all_to_all | solution.py:61
  553.0 21.3 %all-to-all-start.4 = ((bf16[16,3,6144]{2,1,0:T(4,128)(2,1)}), bf16[16,3,6144]{2,1,0:T(4,128)(2,1)S(1)}, u32[]{:S(2)}, u32[]{:S(2)}) async-start(bf16[16,3,6144]{2,1,0:T(4,128)(2,1)} %all_to_all.50), calls=%async_computation.5 | async-start | bytes 1572864 | tf_op jit(solution)/shard_map/all_to_all | solution.py:60
Sparse Core Ops, SparseCore 0:
  32.7 110.5 all-gather.1
  437.0 113.9 reduce-scatter.1
